TPU v7x, 32 devices: a whole 2x2x4 slice. The times are simulated.
32 devices in a mesh: group: 2 (over x), patch: 8 (over z, y), head: 2 (over core).
Axes of the slice: x: 2, y: 2, z: 4, core: 2. Of those that a mesh axis runs over, the one named last changes fastest.
Arguments:
- q_raw: bfloat16 [1536, 1536], P(('group', 'patch', 'head')), parts along dimension 0, may hold values from -2.5 to 2.5
- k_raw: bfloat16 [1536, 1536], P(('group', 'patch', 'head')), parts along dimension 0, may hold values from -2.5 to 2.5
- v_raw: bfloat16 [1536, 1536], P(('group', 'patch', 'head')), parts along dimension 0, may hold values from -6 to 6
- q_gain: float32 [128], replicated, may hold values from 1.5 to 6
- k_gain: float32 [128], replicated, may hold values from 1.5 to 6
- base_kv: bfloat16 [2, 1536, 1536], P(None, 'group', 'head'), parts along dimension 1, may hold values from -6 to 6
- exponents: int32 [2, 12, 16], P(None, None, 'group'), parts along dimension 2, may hold values from -3 to 0
- order: int32 [1536], P('group'), parts along dimension 0, may hold values from 0 to 767, each once
Outputs:
- attn_out: bfloat16 [1536, 1536], P(('group', 'patch', 'head')), parts along dimension 0
There are 2 independent parts, one for each index of `group`. A program takes and returns all parts, laid end to end along the dimension named above; an argument that names none is the same for every part. Nothing has to cross between parts.
Inputs may be any that keep to these rules, and one draw needn't show every extreme that they name: order is a permutation of the 768 positions.
All inputs are finite; a program needn't handle non-finite values.
Results may differ from a plain program's by a relative error of at most 0.003.
The roundings to bfloat16 on the way count: a program that leaves them out, or rounds other values in their place, can miss the bound.
Values may be sent and summed in bfloat16 or wider, within the bound.
A program may use at most 128 MiB of HBM per device.

v0:
```python
import jax
import jax.numpy as jnp
from jax import lax
from jax.sharding import PartitionSpec as P

FH = 16
FW = 16


clip_bound = 8.0
rope_theta = 256.0


def rope_angles(positions, head_size):
    frame_pos = (positions // (FH * FW)).astype(jnp.float32)
    row_pos = (positions // FW % FH).astype(jnp.float32)
    col_pos = (positions % FW).astype(jnp.float32)
    pieces = []
    for coordinate, band_width in (
        (frame_pos, head_size // 8),
        (row_pos, 7 * head_size // 16),
        (col_pos, 7 * head_size // 16),
    ):
        inverse = rope_theta ** (-jnp.arange(0, band_width, 2, dtype=jnp.float32) / band_width)
        pieces.append(coordinate[:, None] * inverse[None, :])
    return jnp.concatenate(pieces, axis=1)


def normed_rotated(raw, gain, positions, head_size):
    count = raw.shape[0]
    values_f = raw.astype(jnp.float32).reshape(count, -1, head_size)
    values_f = (
        values_f * lax.rsqrt(jnp.mean(values_f * values_f, axis=-1, keepdims=True) + 1e-06) * gain
    )
    angles = rope_angles(positions, head_size)[:, None, :]
    paired = values_f.reshape(count, values_f.shape[1], head_size // 2, 2)
    first = paired[..., 0]
    second = paired[..., 1]
    cosine = jnp.cos(angles)
    sine = jnp.sin(angles)
    rotated = jnp.stack([first * cosine - second * sine, first * sine + second * cosine], axis=-1)
    return rotated.reshape(count, -1).astype(jnp.bfloat16)


def head_scores(queries, keys, which, head_size, score_scale):
    query_one = queries[:, which * head_size : (which + 1) * head_size]
    key_one = keys[:, which * head_size : (which + 1) * head_size]
    scores = lax.dot_general(
        query_one, key_one, (((1,), (1,)), ((), ())), preferred_element_type=jnp.float32
    )
    return scores * score_scale


def per_device(q_raw, k_raw, v_raw, q_gain, k_gain, base_kv, exponents, order):
    tok_rows = q_raw.shape[0]
    head_size = q_gain.shape[0]
    head_count = q_raw.shape[1] // head_size
    head_devices = lax.axis_size("head")
    local_heads = head_count // head_devices
    local_width = local_heads * head_size
    patches = exponents.shape[2]
    patch_rows = tok_rows * head_devices
    patch_index = lax.axis_index("patch")
    head_index = lax.axis_index("head")
    patch_start = patch_index * patch_rows
    positions = lax.dynamic_slice_in_dim(order, patch_start, patch_rows)
    stacked = jnp.stack([q_raw, k_raw, v_raw], axis=0)
    moved = lax.all_to_all(stacked, "head", split_axis=2, concat_axis=1, tiled=True)
    queries = normed_rotated(moved[0], q_gain, positions, head_size)
    fresh_keys = normed_rotated(moved[1], k_gain, positions, head_size)
    fresh_values = moved[2]
    base_all = jnp.take(base_kv, order, axis=1)
    base_own = lax.dynamic_slice_in_dim(base_all, patch_start, patch_rows, axis=1)
    base_own = base_own.astype(jnp.float32).reshape(2, patch_rows, local_heads, head_size)
    my_exp = lax.dynamic_slice(
        exponents, (0, head_index * local_heads, 0), (2, local_heads, patches)
    ).astype(jnp.float32)
    send_exp = lax.dynamic_slice_in_dim(my_exp, patch_index, 1, axis=2)[..., 0]
    fresh = (
        jnp.stack([fresh_keys, fresh_values])
        .astype(jnp.float32)
        .reshape(2, patch_rows, local_heads, head_size)
    )
    coded = jnp.clip(
        (fresh - base_own) * jnp.exp2(-send_exp)[:, None, :, None], -clip_bound, clip_bound
    )
    coded = coded.astype(jnp.bfloat16).reshape(2, patch_rows, local_width)
    scale_table = jnp.exp2(my_exp)
    score_scale = head_size ** (-0.5)
    gathered = lax.all_gather(coded, "patch", axis=1, tiled=True)
    count = gathered.shape[1]
    slots = jnp.arange(count, dtype=jnp.int32)
    base_f = base_all.astype(jnp.float32).reshape(2, count, local_heads, head_size)
    owner = slots // patch_rows
    one_hot = (owner[:, None] == jnp.arange(patches, dtype=jnp.int32)[None, :]).astype(jnp.float32)
    row_scale = jnp.sum(one_hot[None, :, None, :] * scale_table[:, None, :, :], axis=-1)
    rebuilt = (
        base_f
        + gathered.reshape(2, count, local_heads, head_size).astype(jnp.float32)
        * row_scale[..., None]
    )
    rebuilt = rebuilt.astype(jnp.bfloat16).reshape(2, count, local_width)
    keys = rebuilt[0]
    values = rebuilt[1]
    results = []
    for which in range(local_heads):
        scores = head_scores(queries, keys, which, head_size, score_scale)
        row_max = jnp.max(scores, axis=-1, keepdims=True)
        weights = jnp.exp(scores - row_max)
        row_total = jnp.sum(weights, axis=-1, keepdims=True)
        value_one = values[:, which * head_size : (which + 1) * head_size]
        accum = jnp.dot(weights.astype(jnp.bfloat16), value_one, preferred_element_type=jnp.float32)
        results.append((accum / row_total).astype(jnp.bfloat16))
    attended = jnp.concatenate(results, axis=1)
    return lax.all_to_all(attended, "head", split_axis=0, concat_axis=1, tiled=True)


def solution(mesh):
    in_specs = (
        P(("group", "patch", "head"), None),
        P(("group", "patch", "head"), None),
        P(("group", "patch", "head"), None),
        P(),
        P(),
        P(None, "group", "head"),
        P(None, None, "group"),
        P("group"),
    )
    out_specs = P(("group", "patch", "head"), None)
    return jax.shard_map(
        per_device, mesh=mesh, in_specs=in_specs, out_specs=out_specs, check_vma=False
    )
```

profile of v0, /device:TPU:0, one launch (start us, length us, event | category | flops | bytes accessed | tf_op | source)
XLA Modules:
  0.0 132.1 jit_solution(8788164474265471336)
XLA Ops:
  6.5 1.3 pad_maximum_fusion
  7.8 2.2 %copy.55 = bf16[3,48,1536]{1,0,2:T(4,128)(2,1)} copy(bf16[3,48,1536]{2,1,0:T(8,128)(2,1)S(1)} %pad_maximum_fusion) | data formatting | bytes 884736 | tf_op jit(solution)/shard_map/stack | solution.py:67
  10.0 3.6 %reshape.254 = bf16[2,2,55296]{2,1,0:T(2,128)(2,1)} reshape(bf16[1536,3,48]{2,1,0:T(4,128)(2,1)} %bitcast.37) | data formatting | bytes 884736
  13.6 3.5 %all-to-all-start = ((bf16[2,2,55296]{2,1,0:T(2,128)(2,1)}), bf16[2,2,55296]{2,1,0:T(2,128)(2,1)S(1)}, u32[]{:S(2)}, u32[]{:S(2)}) async-start(bf16[2,2,55296]{2,1,0:T(2,128)(2,1)} %reshape.254), calls=%async_computation | async-start | bytes 884736 | tf_op jit(solution)/shard_map/all_to_all | solution.py:68
  17.1 0.6 multiply_power_fusion.1
  17.7 0.6 multiply_power_fusion
  18.3 0.4 all-to-all-done
  18.7 2.9 %reshape.255 = bf16[1536,3,48]{2,1,0:T(4,128)(2,1)} reshape(bf16[2,2,55296]{2,1,0:T(2,128)(2,1)S(1)} %all-to-all-done) | data formatting | bytes 884736
  21.7 2.5 %copy.56 = bf16[3,48,2,768]{3,1,2,0:T(8,128)(2,1)S(1)} copy(bf16[3,48,2,768]{1,0,3,2:T(4,128)(2,1)} %bitcast.38) | data formatting | bytes 884736 | tf_op jit(solution)/shard_map/all_to_all | solution.py:68
  24.3 0.9 slice_convert_fusion.1
  25.2 0.7 fusion.62
  25.8 0.6 dynamic-slice
  26.4 0.5 fusion.63
  26.9 0.6 pad_clamp_fusion
  27.7 0.8 mul.271
  28.4 0.7 mul.295
  29.5 0.6 add_rsqrt_fusion.1
  30.4 0.6 add_rsqrt_fusion
  31.0 0.5 copy.57
  31.5 0.7 reshape.242
  32.2 1.3 %copy.60 = f32[1,2,48,768]{2,1,3,0:T(2,128)S(1)} copy(f32[1,2,48,768]{3,2,1,0:T(8,128)} %get-tuple-element.19) | data formatting | bytes 589824 | tf_op jit(solution)/shard_map/convert_element_type | solution.py:31
  33.5 1.4 %reshape.243 = f32[96,6,64,2]{0,3,2,1:T(2,128)} reshape(f32[1,2,48,768]{2,1,3,0:T(2,128)S(1)} %copy.60) | data formatting | bytes 589824 | tf_op jit(solution)/shard_map/convert_element_type | solution.py:31
  35.0 0.8 broadcast_multiply_fusion.2
  35.8 0.7 broadcast_multiply_fusion.1
  36.7 1.0 multiply_multiply_fusion.1
  37.7 1.0 multiply_multiply_fusion
  38.7 1.0 subtract_convert_fusion.1
  39.7 1.0 pad_maximum_fusion.1
  40.9 9.4 %gather_fusion = bf16[768,2,768]{2,0,1:T(8,128)(2,1)} fusion(bf16[2,768,768]{2,1,0:T(8,128)(2,1)S(1)} %copy-done, s32[1024]{0:T(1024)S(1)} %copy-done.5), kind=kCustom, calls=%fused_computation | custom fusion | bytes 4721664 | tf_op jit(solution)/shard_map/jit(_take)/gather | solution.py:72
  50.3 1.9 %clamp_convert_fusion = bf16[2,96,768]{2,1,0:T(8,128)(2,1)} fusion(bf16[2,768,768]{2,1,0:T(8,128)(2,1)} %bitcast.34, s32[]{:T(128)S(6)} %select_n.55, bf16[1,96,768]{2,1,0:T(8,128)(2,1)S(1)} %bitcast.60, bf16[1,96,768]{2,1,0:T(8,128)(2,1)S(1)} %copy.62, f32[2,768]{1,0:T(2,128)S(1)} %bitcast.66, pred[96]{0:T(512)(128)(4,1)S(1)} %copy-done.11), kind=kLoop, calls=%fused_computation.26 | loop fusion | flops 1474560 | bytes 890980 | tf_op jit(solution)/shard_map/convert_element_type | solution.py:87
  52.2 4.3 %copy.59 = bf16[2,768,768]{1,2,0:T(8,128)(2,1)} copy(bf16[2,768,768]{2,1,0:T(8,128)(2,1)} %bitcast.35) | data formatting | bytes 4718592 | tf_op jit(solution)/shard_map/jit(_take)/gather | solution.py:72
  56.8 50.4 %all-gather.2.cloned.1.call-done = bf16[2,768,768]{2,1,0:T(8,128)(2,1)} async-done(((bf16[2,96,768]{2,1,0:T(8,128)(2,1)}), bf16[2,768,768]{2,1,0:T(8,128)(2,1)}) %all-gather.2.cloned.1.call-update) | async-done | bytes 2359312 | tf_op jit(solution)/shard_map/all_gather | solution.py:90
  107.2 4.6 %copy.63 = f32[2,768,768]{1,2,0:T(8,128)} copy(bf16[2,768,768]{2,1,0:T(8,128)(2,1)} %all-gather.2.cloned.1.call-done) | data formatting | bytes 7077888 | tf_op jit(solution)/shard_map/convert_element_type | solution.py:99
  111.8 3.8 %add_convert_fusion = bf16[2,768,6,128]{1,3,2,0:T(8,128)(2,1)S(1)} fusion(f32[2,768,6,128]{1,3,2,0:T(8,128)} %bitcast.33, f32[2,768,6]{1,2,0:T(8,128)S(1)} %multiply_reduce_fusion, bf16[2,768,6,128]{1,3,2,0:T(8,128)(2,1)} %bitcast.36, pred[768]{0:T(1024)(128)(4,1)S(1)} %copy-done.8), kind=kLoop, calls=%fused_computation.1 | loop fusion | flops 5898240 | bytes 9474816 | tf_op jit(solution)/shard_map/convert_element_type | solution.py:102
  115.8 0.3 fusion.72
  116.1 0.3 fusion.71
  116.4 0.3 fusion.70
  116.8 0.3 fusion.69
  117.1 0.3 fusion.68
  117.4 0.3 fusion.67
  119.0 0.3 fusion.1
  119.3 0.3 fusion.3
  119.6 0.3 fusion.5
  119.9 0.3 fusion.7
  120.2 0.3 fusion.9
  120.4 0.3 fusion.11
  120.7 3.8 %all_to_all.34 = bf16[2,48,768]{2,1,0:T(8,128)(2,1)S(1)} all-to-all(bf16[2,48,768]{2,1,0:T(8,128)(2,1)S(1)} %bitcast.65), channel_id=1, replica_groups=mesh['group'=2,'patch'=8,'head'=2] {'head'}, dimensions={0} | all-to-all | bytes 294912 | tf_op jit(solution)/shard_map/all_to_all | solution.py:115
  124.5 0.7 copy.66
  (52 shorter events, 2.9 us)
Async XLA Ops:
  6.5 34.4 %copy-start = (bf16[2,768,768]{2,1,0:T(8,128)(2,1)S(1)}, bf16[2,768,768]{2,1,0:T(8,128)(2,1)}, u32[]{:S(2)}) copy-start(bf16[2,768,768]{2,1,0:T(8,128)(2,1)} %param.13) | copy-start | bytes 7077892
  10.0 8.3 %copy-start.4 = (s32[768]{0:T(1024)S(1)}, s32[768]{0:T(1024)}, u32[]{:S(2)}) copy-start(s32[768]{0:T(1024)} %param.15) | copy-start | bytes 9220
  13.6 5.2 %all-to-all-start = ((bf16[2,2,55296]{2,1,0:T(2,128)(2,1)}), bf16[2,2,55296]{2,1,0:T(2,128)(2,1)S(1)}, u32[]{:S(2)}, u32[]{:S(2)}) async-start(bf16[2,2,55296]{2,1,0:T(2,128)(2,1)} %reshape.254), calls=%async_computation | async-start | bytes 884736 | tf_op jit(solution)/shard_map/all_to_all | solution.py:68
  17.1 90.1 %all-gather.2.cloned.1.call-start = ((), (), s32[]{:S(2)}) async-start(), calls=%async_computation.2 | async-start | bytes 2654208 | tf_op jit(solution)/shard_map/all_gather | solution.py:90
  18.3 7.5 %copy-start.7 = (pred[768]{0:T(1024)(128)(4,1)}, pred[768]{0:T(1024)(128)(4,1)S(1)}, u32[]{:S(2)}) copy-start(pred[768]{0:T(1024)(128)(4,1)S(1)} %compare_and_fusion) | copy-start | bytes 2308
  24.2 3.3 %copy-start.6 = (s32[2,12,8]{1,2,0:T(8,128)S(1)}, s32[2,12,8]{1,2,0:T(8,128)}, u32[]{:S(2)}) copy-start(s32[2,12,8]{1,2,0:T(8,128)} %param.14) | copy-start | bytes 2308
  24.2 3.5 %copy-start.9 = (f32[128]{0:T(128)S(1)}, f32[128]{0:T(128)}, u32[]{:S(2)}) copy-start(f32[128]{0:T(128)} %param.11) | copy-start | bytes 1540
  24.2 4.2 %copy-start.10 = (f32[128]{0:T(128)S(1)}, f32[128]{0:T(128)}, u32[]{:S(2)}) copy-start(f32[128]{0:T(128)} %param.12) | copy-start | bytes 1540
  29.2 1.8 %copy-start.2 = (f32[1,2,48,768]{3,2,1,0:T(8,128)S(1)}, f32[1,2,48,768]{3,2,1,0:T(8,128)}, u32[]{:S(2)}) copy-start(f32[1,2,48,768]{3,2,1,0:T(8,128)} %get-tuple-element.17) | copy-start | bytes 884740
  35.0 2.7 %copy-start.1 = (f32[96,6,64,2]{0,3,2,1:T(2,128)S(1)}, f32[96,6,64,2]{0,3,2,1:T(2,128)}, u32[]{:S(2)}) copy-start(f32[96,6,64,2]{0,3,2,1:T(2,128)} %reshape.243) | copy-start | bytes 884740
  38.7 2.2 %copy-start.5 = (s32[1024]{0:T(1024)S(1)}, s32[1024]{0:T(1024)}, u32[]{:S(2)}) copy-start(s32[1024]{0:T(1024)} %pad_clamp_fusion) | copy-start | bytes 12292
  40.9 9.4 %copy-start.3 = (bf16[1,2,48,768]{3,2,1,0:T(8,128)(2,1)S(1)}, bf16[1,2,48,768]{3,2,1,0:T(8,128)(2,1)}, u32[]{:S(2)}) copy-start(bf16[1,2,48,768]{3,2,1,0:T(8,128)(2,1)} %get-tuple-element.18) | copy-start | bytes 442372
  40.9 9.4 %copy-start.11 = (pred[96]{0:T(512)(128)(4,1)S(1)}, pred[96]{0:T(512)(128)(4,1)}, u32[]{:S(2)}) copy-start(pred[96]{0:T(512)(128)(4,1)} %dynamic-slice) | copy-start | bytes 292
  56.8 55.0 %copy-start.8 = (pred[768]{0:T(1024)(128)(4,1)S(1)}, pred[768]{0:T(1024)(128)(4,1)}, u32[]{:S(2)}) copy-start(pred[768]{0:T(1024)(128)(4,1)} %copy-done.7) | copy-start | bytes 2308
Sparse Core Ops, SparseCore 0:
  52.4 54.7 all-gather.1
where the time goes:
time: 133 us; the launch traced here: 132 us
  waiting for transfers between devices  50.8 us (38%)
  local copies, waits for them, and re-layouts  37 us (28%)
  other arithmetic  19.6 us (15%)
  between operations  13.8 us (10%)
  blocking collectives  3.82 us (3%)
  matrix products  3.57 us (3%)
  starting transfers between devices  3.51 us (3%)
    all_gather x1, waiting for transfers between devices, per_device(): gathered = lax.all_gather(coded, 'patch', axis=1, tiled=True)  50.4 us
    gather x2, local copies, waits for them, and re-layouts, per_device(): base_all = jnp.take(base_kv, order, axis=1)  13.7 us
    unnamed x28, local copies, waits for them, and re-layouts  6.66 us
    convert_element_type x1, local copies, waits for them, and re-layouts, per_device(): gathered.reshape(2, count, local_heads, head_size).astype(jnp.float32)  4.57 us
    convert_element_type x4, local copies, waits for them, and re-layouts, normed_rotated(): values_f = raw.astype(jnp.float32).reshape(count, -1, head_size)  3.96 us
    convert_element_type x1, other arithmetic, per_device(): rebuilt = rebuilt.astype(jnp.bfloat16).reshape(2, count, local_width)  3.84 us
    all_to_all x1, blocking collectives, per_device(): lax.all_to_all(attended, 'head', split_axis=0, concat_axis=1, tiled=True)  3.82 us
    all_to_all x1, starting transfers between devices, per_device(): lax.all_to_all(stacked, 'head', split_axis=2, concat_axis=1, tiled=True)  3.47 us
  transfers between devices with their start and end apart: 2, of which 2 were waited for; matrix products, arithmetic and copies ran while one was open for 4% of the time, Pallas kernels for 0%

commit v1 on v0

v1 whole, which is shorter than its diff:
```python
import functools

import jax
import jax.numpy as jnp
from jax import lax
from jax.experimental import pallas as pl
from jax.experimental.pallas import tpu as pltpu
from jax.sharding import PartitionSpec as P

FH = 16
FW = 16
LANES = 128

clip_bound = 8.0
rope_theta = 256.0


def kernel(
    sizes, q_ref, k_ref, v_ref, qg_ref, kg_ref, exp_ref, order_ref, base_ref, out_ref,
    send_buf, recv_buf, base_buf, pos_buf, slot_base, cos_buf, sin_buf,
    q_buf, key_buf, val_buf, o_send, o_recv,
    base_sem, send_sem, recv_sem, osend_sem, orecv_sem,
):
    n, cores, local_heads, rows = sizes
    blocks = n * cores
    heads = local_heads * cores
    hd = LANES
    tokens = blocks * rows
    patch_rows = cores * rows
    first_worker = (n - local_heads) // 2
    patch = lax.axis_index("patch")
    core = lax.axis_index("head")
    me = patch * cores + core
    local_head = patch - first_worker
    is_worker = jnp.logical_and(local_head >= 0, local_head < local_heads)
    my_head = core * local_heads + local_head

    def block_device(block):
        return {"patch": block // cores, "head": block % cores}

    def head_device(head):
        return {"patch": first_worker + head % local_heads, "head": head // local_heads}

    def in_copy(head, block):
        return pltpu.make_async_remote_copy(
            src_ref=send_buf.at[head],
            dst_ref=recv_buf.at[block],
            send_sem=send_sem.at[head],
            recv_sem=recv_sem.at[block],
            device_id=head_device(head),
            device_id_type=pl.DeviceIdType.MESH,
        )

    def out_copy(block, head):
        return pltpu.make_async_remote_copy(
            src_ref=o_send.at[block],
            dst_ref=o_recv.at[head],
            send_sem=osend_sem.at[block],
            recv_sem=orecv_sem.at[head],
            device_id=block_device(block),
            device_id_type=pl.DeviceIdType.MESH,
        )

    def base_copy(which):
        column = pl.multiple_of(local_head * hd, hd)
        return pltpu.make_async_copy(
            base_ref.at[which, :, pl.ds(column, hd)],
            base_buf.at[:, pl.ds(which * hd, hd)],
            base_sem.at[which],
        )

    barrier = pltpu.get_barrier_semaphore()

    @pl.loop(1, blocks)
    def _(step):
        pl.semaphore_signal(
            barrier, inc=1, device_id=block_device((me + step) % blocks),
            device_id_type=pl.DeviceIdType.MESH,
        )

    @pl.when(is_worker)
    def _():
        base_copy(0).start()
        base_copy(1).start()

    for head in range(heads):
        column = slice(head * hd, (head + 1) * hd)
        send_buf[head, 0] = k_ref[:, column]
        send_buf[head, 1] = v_ref[:, column]
        send_buf[head, 2] = q_ref[:, column]

    @pl.when(is_worker)
    def _():
        recv_buf[me] = send_buf[my_head]

    pl.semaphore_wait(barrier, blocks - 1)

    def is_mine(head):
        return jnp.logical_and(is_worker, head == my_head)

    @pl.loop(0, heads)
    def _(step):
        head = (me + step) % heads

        @pl.when(jnp.logical_not(is_mine(head)))
        def _():
            in_copy(head, me).start()

    @pl.when(is_worker)
    def _():
        lane = lax.broadcasted_iota(jnp.int32, (1, hd), 1)
        pair = lane // 2
        even = lane % 2 == 0
        band = hd // 16
        wide = (hd // 2 - band) // 2
        in_frame = pair < band
        in_row = pair < band + wide
        start = jnp.where(in_frame, 0, jnp.where(in_row, band, band + wide))
        width = jnp.where(in_frame, float(band), float(wide))
        ratio = (pair - start).astype(jnp.float32) / width
        inverse = jnp.exp(ratio * (-5.545177444479562))
        for j in range(tokens // LANES):
            piece = order_ref[:, j * LANES : (j + 1) * LANES]
            pos_buf[j * LANES : (j + 1) * LANES, :] = jnp.transpose(
                jnp.broadcast_to(piece, (LANES, LANES))
            )
        base_copy(0).wait()
        base_copy(1).wait()

        @pl.loop(0, n)
        def _(b):
            where = pl.ds(pl.multiple_of(b * patch_rows, 16), patch_rows)
            pos = pos_buf[where, :]
            one_hot = jnp.concatenate(
                [
                    jnp.where(pos == lane + j * LANES, 1.0, 0.0).astype(jnp.bfloat16)
                    for j in range(tokens // LANES)
                ],
                axis=1,
            )
            slot_base[where, :] = jnp.dot(
                one_hot, base_buf[...], preferred_element_type=jnp.float32
            )
            coordinate = jnp.where(
                in_frame,
                pos // (FH * FW),
                jnp.where(in_row, pos // FW % FH, pos % FW),
            ).astype(jnp.float32)
            angles = coordinate * inverse
            sine = jnp.sin(angles)
            cos_buf[where, :] = jnp.cos(angles)
            sin_buf[where, :] = jnp.where(even, -sine, sine)

        def normed_rotated(raw, gain, cosine, sine):
            mean = jnp.sum(raw * raw, axis=-1, keepdims=True) * (1.0 / hd)
            x = raw * lax.rsqrt(mean + 1e-06) * gain
            swapped = jnp.where(even, pltpu.roll(x, hd - 1, 1), pltpu.roll(x, 1, 1))
            return (x * cosine + swapped * sine).astype(jnp.bfloat16)

        def rebuilt(fresh, base, exponent):
            power = jnp.full((1, hd), exponent, jnp.int32).astype(jnp.float32)
            coded = jnp.clip((fresh - base) * jnp.exp2(-power), -clip_bound, clip_bound)
            coded = coded.astype(jnp.bfloat16).astype(jnp.float32)
            return (base + coded * jnp.exp2(power)).astype(jnp.bfloat16)

        @pl.loop(0, n)
        def _(b):
            for c in range(cores):
                block = b * cores + c

                @pl.when(block != me)
                def _():
                    in_copy(my_head, block).wait_recv()

                where = pl.ds(pl.multiple_of(block * rows, 16), rows)
                cosine = cos_buf[where, :]
                sine = sin_buf[where, :]
                k_raw = recv_buf[block, 0].astype(jnp.float32)
                v_raw = recv_buf[block, 1].astype(jnp.float32)
                q_raw = recv_buf[block, 2].astype(jnp.float32)
                q_buf[where, :] = normed_rotated(q_raw, qg_ref[...], cosine, sine)
                fresh = normed_rotated(k_raw, kg_ref[...], cosine, sine).astype(jnp.float32)
                key_buf[where, :] = rebuilt(
                    fresh, slot_base[where, :hd], exp_ref[0, my_head, b]
                )
                val_buf[where, :] = rebuilt(
                    v_raw, slot_base[where, hd:], exp_ref[1, my_head, b]
                )

        tile = 2 * patch_rows
        per_tile = tile // rows
        score_scale = hd ** (-0.5)

        @pl.loop(0, tokens // tile)
        def _(t):
            where = pl.ds(pl.multiple_of(t * tile, 16), tile)
            scores = lax.dot_general(
                q_buf[where, :], key_buf[...], (((1,), (1,)), ((), ())),
                preferred_element_type=jnp.float32,
            ) * score_scale
            weights = jnp.exp(scores - jnp.max(scores, axis=-1, keepdims=True))
            total = jnp.sum(weights, axis=-1, keepdims=True)
            accum = jnp.dot(
                weights.astype(jnp.bfloat16), val_buf[...], preferred_element_type=jnp.float32
            )
            result = (accum / total).astype(jnp.bfloat16)
            for i in range(per_tile):
                block = t * per_tile + i
                o_send[block] = result[i * rows : (i + 1) * rows]

                @pl.when(block != me)
                def _():
                    out_copy(block, my_head).start()

        o_recv[my_head] = o_send[me]

    for head in range(heads):
        @pl.when(jnp.logical_not(is_mine(head)))
        def _():
            out_copy(me, head).wait_recv()

        out_ref[:, head * hd : (head + 1) * hd] = o_recv[head]

    @pl.loop(0, heads)
    def _(head):
        @pl.when(jnp.logical_not(is_mine(head)))
        def _():
            in_copy(head, me).wait_send()

    @pl.when(is_worker)
    def _():
        @pl.loop(0, blocks)
        def _(block):
            @pl.when(block != me)
            def _():
                out_copy(block, my_head).wait_send()


def per_device(q_raw, k_raw, v_raw, q_gain, k_gain, base_kv, exponents, order):
    rows = q_raw.shape[0]
    hd = q_gain.shape[0]
    heads = q_raw.shape[1] // hd
    n = lax.axis_size("patch")
    cores = lax.axis_size("head")
    blocks = n * cores
    tokens = blocks * rows
    vmem = pl.BlockSpec(memory_space=pltpu.VMEM)
    return pl.pallas_call(
        functools.partial(kernel, (n, cores, heads // cores, rows)),
        out_shape=jax.ShapeDtypeStruct(q_raw.shape, jnp.bfloat16),
        in_specs=[vmem] * 5
        + [pl.BlockSpec(memory_space=pltpu.SMEM), vmem, pl.BlockSpec(memory_space=pl.ANY)],
        out_specs=vmem,
        scratch_shapes=[
            pltpu.VMEM((heads, 3, rows, hd), jnp.bfloat16),
            pltpu.VMEM((blocks, 3, rows, hd), jnp.bfloat16),
            pltpu.VMEM((tokens, 2 * hd), jnp.bfloat16),
            pltpu.VMEM((tokens, hd), jnp.int32),
            pltpu.VMEM((tokens, 2 * hd), jnp.float32),
            pltpu.VMEM((tokens, hd), jnp.float32),
            pltpu.VMEM((tokens, hd), jnp.float32),
            pltpu.VMEM((tokens, hd), jnp.bfloat16),
            pltpu.VMEM((tokens, hd), jnp.bfloat16),
            pltpu.VMEM((tokens, hd), jnp.bfloat16),
            pltpu.VMEM((blocks, rows, hd), jnp.bfloat16),
            pltpu.VMEM((heads, rows, hd), jnp.bfloat16),
            pltpu.SemaphoreType.DMA((2,)),
            pltpu.SemaphoreType.DMA((heads,)),
            pltpu.SemaphoreType.DMA((blocks,)),
            pltpu.SemaphoreType.DMA((blocks,)),
            pltpu.SemaphoreType.DMA((heads,)),
        ],
        compiler_params=pltpu.CompilerParams(
            collective_id=0, has_side_effects=True, vmem_limit_bytes=40 * 2**20
        ),
    )(
        q_raw, k_raw, v_raw, q_gain.reshape(1, hd), k_gain.reshape(1, hd), exponents,
        order.reshape(1, tokens), base_kv,
    )


def solution(mesh):
    in_specs = (
        P(("group", "patch", "head"), None),
        P(("group", "patch", "head"), None),
        P(("group", "patch", "head"), None),
        P(),
        P(),
        P(None, "group", "head"),
        P(None, None, "group"),
        P("group"),
    )
    out_specs = P(("group", "patch", "head"), None)
    return jax.shard_map(
        per_device, mesh=mesh, in_specs=in_specs, out_specs=out_specs, check_vma=False
    )
```

time: 133 us -> 33.7 us (0.25)
  waiting for transfers between devices: 50.8 us -> 0 us
  local copies, waits for them, and re-layouts: 37 us -> 7.84 us
  Pallas kernels: 0 us -> 25.3 us
  other arithmetic: 19.6 us -> 0 us
  between operations: 13.8 us -> 0.02 us
  blocking collectives: 3.82 us -> 0 us
  matrix products: 3.57 us -> 0 us
  starting transfers between devices: 3.51 us -> 0 us
    all_gather x1 -> x0, waiting for transfers between devices: 50.4 us -> none  [per_device(): gathered = lax.all_gather(coded, 'patch', axis=1, tiled=True)]
    pallas_call x0 -> x1, Pallas kernels: none -> 25.3 us  [per_device(): pl.pallas_call(functools.partial(kernel, (n, cores, heads // cores, rows)...]
    gather x2 -> x0, local copies, waits for them, and re-layouts: 13.7 us -> none  [per_device(): base_all = jnp.take(base_kv, order, axis=1)]
    convert_element_type x6 -> x0, local copies, waits for them, and re-layouts: 8.67 us -> none  [the longest x1 4.57 us: per_device(): gathered.reshape(2, count, local_heads, head_size).astype(jnp.float32)]
    convert_element_type x6 -> x0, other arithmetic: 7.77 us -> none  [the longest x1 3.84 us: per_device(): rebuilt = rebuilt.astype(jnp.bfloat16).reshape(2, count, local_width)]
    all_to_all x1 -> x0, blocking collectives: 3.82 us -> none  [per_device(): lax.all_to_all(attended, 'head', split_axis=0, concat_axis=1, tiled=True)]
    dot_general x12 -> x0, matrix products: 3.57 us -> none  [the longest x6 1.94 us: head_scores(): lax.dot_general(query_one, key_one, (((1,), (1,)), ((), ())), preferred_e...]
    mul x5 -> x0, other arithmetic: 3.55 us -> none  [the longest x2 1.96 us: normed_rotated(): values_f * lax.rsqrt(jnp.mean(values_f * values_f, axis=-1, keepdims=True...]
  transfers between devices with their start and end apart: 2 -> 0, of which waited for: 2 -> 0; matrix products, arithmetic and copies ran while one was open for 4% -> 0% of each run, Pallas kernels for 0% -> 0%
where the time goes in v1:
time: 33.7 us; the launch traced here: 33.2 us
  Pallas kernels  25.3 us (75%)
  local copies, waits for them, and re-layouts  7.84 us (23%)
    pallas_call x1, Pallas kernels, per_device(): pl.pallas_call(functools.partial(kernel, (n, cores, heads // cores, rows)...  25.3 us
    unnamed x14, local copies, waits for them, and re-layouts  7.15 us
    reshape x1, local copies, waits for them, and re-layouts, per_device(): order.reshape(1, tokens)  0.69 us

profile of v1, /device:TPU:0, one launch (start us, length us, event | category | flops | bytes accessed | tf_op | source)
XLA Modules:
  0.0 33.2 jit_solution(10046619357960854522)
XLA Ops:
  0.0 0.7 %reshape.11.order_ref = s32[1,768]{1,0:T(1,128)S(1)} reshape(s32[768]{0:T(1024)} %param.15) | data formatting | bytes 6144 | tf_op jit(solution)/shard_map/reshape | solution.py:278
  0.7 0.8 %copy.9.exp_ref = s32[2,12,8]{2,1,0:T(8,128)S(1)} copy(s32[2,12,8]{1,2,0:T(8,128)} %param.14) | data formatting | bytes 1536 | tf_op args[6]
  1.5 0.0 copy-start
  1.5 1.7 %copy-done = bf16[2,768,768]{2,1,0:T(8,128)(2,1)S(1)} copy-done((bf16[2,768,768]{2,1,0:T(8,128)(2,1)S(1)}, bf16[2,768,768]{2,1,0:T(8,128)(2,1)}, u32[]{:S(2)}) %copy-start) | copy-done | bytes 2359320
  3.1 0.0 copy-start.1
  3.1 0.9 %copy-done.1 = bf16[48,1536]{1,0:T(8,128)(2,1)S(1)} copy-done((bf16[48,1536]{1,0:T(8,128)(2,1)S(1)}, bf16[48,1536]{1,0:T(8,128)(2,1)}, u32[]{:S(2)}) %copy-start.1) | copy-done | bytes 147480
  4.1 0.0 copy-start.2
  4.1 0.9 %copy-done.2 = bf16[48,1536]{1,0:T(8,128)(2,1)S(1)} copy-done((bf16[48,1536]{1,0:T(8,128)(2,1)S(1)}, bf16[48,1536]{1,0:T(8,128)(2,1)}, u32[]{:S(2)}) %copy-start.2) | copy-done | bytes 147480
  5.0 0.0 copy-start.3
  5.0 0.9 %copy-done.3 = bf16[48,1536]{1,0:T(8,128)(2,1)S(1)} copy-done((bf16[48,1536]{1,0:T(8,128)(2,1)S(1)}, bf16[48,1536]{1,0:T(8,128)(2,1)}, u32[]{:S(2)}) %copy-start.3) | copy-done | bytes 147480
  5.9 0.0 copy-start.4
  5.9 0.7 %copy-done.4 = f32[128]{0:T(128)S(1)} copy-done((f32[128]{0:T(128)S(1)}, f32[128]{0:T(128)}, u32[]{:S(2)}) %copy-start.4) | copy-done | bytes 536
  6.5 0.0 copy-start.5
  6.5 0.7 %copy-done.5 = f32[128]{0:T(128)S(1)} copy-done((f32[128]{0:T(128)S(1)}, f32[128]{0:T(128)}, u32[]{:S(2)}) %copy-start.5) | copy-done | bytes 536
  7.2 25.3 %shard_map.82 = bf16[48,1536]{1,0:T(8,128)(2,1)S(1)} custom-call(bf16[48,1536]{1,0:T(8,128)(2,1)S(1)} %copy-done.1, bf16[48,1536]{1,0:T(8,128)(2,1)S(1)} %copy-done.2, bf16[48,1536]{1,0:T(8,128)(2,1)S(1)} %copy-done.3, f32[1,128]{1,0:T(1,128)S(1)} %bitcast.2, f32[1,128]{1,0:T(1,128)S(1)} %bitcast.3, s32[2,12,8]{2,1,0:T(8,128)S(1)} %copy.9.exp_ref, ...), custom_call_target="tpu_custom_call" | custom-call | tf_op jit(solution)/shard_map/pallas_call | solution.py:248
  32.5 0.7 %copy.11 = bf16[48,1536]{1,0:T(8,128)(2,1)} copy(bf16[48,1536]{1,0:T(8,128)(2,1)S(1)} %shard_map.82) | data formatting | bytes 294912
Async XLA Ops:
  1.5 1.7 %copy-start = (bf16[2,768,768]{2,1,0:T(8,128)(2,1)S(1)}, bf16[2,768,768]{2,1,0:T(8,128)(2,1)}, u32[]{:S(2)}) copy-start(bf16[2,768,768]{2,1,0:T(8,128)(2,1)} %base_ref.1) | copy-start | bytes 7077892
  3.1 0.9 %copy-start.1 = (bf16[48,1536]{1,0:T(8,128)(2,1)S(1)}, bf16[48,1536]{1,0:T(8,128)(2,1)}, u32[]{:S(2)}) copy-start(bf16[48,1536]{1,0:T(8,128)(2,1)} %q_ref.1) | copy-start | bytes 442372
  4.1 0.9 %copy-start.2 = (bf16[48,1536]{1,0:T(8,128)(2,1)S(1)}, bf16[48,1536]{1,0:T(8,128)(2,1)}, u32[]{:S(2)}) copy-start(bf16[48,1536]{1,0:T(8,128)(2,1)} %k_ref.1) | copy-start | bytes 442372
  5.0 0.9 %copy-start.3 = (bf16[48,1536]{1,0:T(8,128)(2,1)S(1)}, bf16[48,1536]{1,0:T(8,128)(2,1)}, u32[]{:S(2)}) copy-start(bf16[48,1536]{1,0:T(8,128)(2,1)} %v_ref.1) | copy-start | bytes 442372
  5.9 0.7 %copy-start.4 = (f32[128]{0:T(128)S(1)}, f32[128]{0:T(128)}, u32[]{:S(2)}) copy-start(f32[128]{0:T(128)} %param.11) | copy-start | bytes 1540
  6.5 0.7 %copy-start.5 = (f32[128]{0:T(128)S(1)}, f32[128]{0:T(128)}, u32[]{:S(2)}) copy-start(f32[128]{0:T(128)} %param.12) | copy-start | bytes 1540

commit v2 on v1

--- a/solution.py
+++ b/solution.py
@@ -17,9 +17,9 @@
 
 def kernel(
     sizes, q_ref, k_ref, v_ref, qg_ref, kg_ref, exp_ref, order_ref, base_ref, out_ref,
-    send_buf, recv_buf, base_buf, pos_buf, slot_base, cos_buf, sin_buf,
+    raw_buf, gain_buf, exp_buf, order_buf, scale_buf, send_buf, recv_buf, base_buf, pos_buf, slot_base, cos_buf, sin_buf,
     q_buf, key_buf, val_buf, o_send, o_recv,
-    base_sem, send_sem, recv_sem, osend_sem, orecv_sem,
+    in_sem, small_sem, base_sem, send_sem, recv_sem, osend_sem, orecv_sem,
 ):
     n, cores, local_heads, rows = sizes
     blocks = n * cores
@@ -69,6 +69,24 @@
             base_sem.at[which],
         )
 
+    in_copies = [
+        pltpu.make_async_copy(ref, raw_buf.at[i], in_sem.at[i])
+        for i, ref in enumerate((k_ref, v_ref, q_ref))
+    ]
+    small_copies = [
+        pltpu.make_async_copy(src, dst, small_sem.at[i])
+        for i, (src, dst) in enumerate(
+            (
+                (order_ref, order_buf),
+                (exp_ref, exp_buf),
+                (qg_ref, gain_buf.at[0]),
+                (kg_ref, gain_buf.at[1]),
+            )
+        )
+    ]
+    for copy in in_copies:
+        copy.start()
+
     barrier = pltpu.get_barrier_semaphore()
 
     @pl.loop(1, blocks)
@@ -80,14 +98,15 @@
 
     @pl.when(is_worker)
     def _():
+        for copy in small_copies:
+            copy.start()
         base_copy(0).start()
         base_copy(1).start()
 
-    for head in range(heads):
-        column = slice(head * hd, (head + 1) * hd)
-        send_buf[head, 0] = k_ref[:, column]
-        send_buf[head, 1] = v_ref[:, column]
-        send_buf[head, 2] = q_ref[:, column]
+    for i, copy in enumerate(in_copies):
+        copy.wait()
+        for head in range(heads):
+            send_buf[head, i] = raw_buf[i, :, head * hd : (head + 1) * hd]
 
     @pl.when(is_worker)
     def _():
@@ -98,13 +117,20 @@
     def is_mine(head):
         return jnp.logical_and(is_worker, head == my_head)
 
-    @pl.loop(0, heads)
-    def _(step):
-        head = (me + step) % heads
-
-        @pl.when(jnp.logical_not(is_mine(head)))
-        def _():
-            in_copy(head, me).start()
+    lower = patch < n // 2
+    half_heads = local_heads // 2
+    for step in range(local_heads):
+        if local_heads % 2 == 0:
+            across = (step < half_heads) == lower
+            target = (patch + step) % half_heads + jnp.where(across, half_heads, 0)
+        else:
+            target = (patch + step) % local_heads
+        for c in range(cores):
+            head = ((core + c) % cores) * local_heads + target
+
+            @pl.when(jnp.logical_not(is_mine(head)))
+            def _():
+                in_copy(head, me).start()
 
     @pl.when(is_worker)
     def _():
@@ -119,8 +145,18 @@
         width = jnp.where(in_frame, float(band), float(wide))
         ratio = (pair - start).astype(jnp.float32) / width
         inverse = jnp.exp(ratio * (-5.545177444479562))
+        for copy in small_copies:
+            copy.wait()
+        for which in range(2):
+            mine = lax.broadcasted_iota(jnp.int32, (n, heads), 1) == my_head
+            power = jnp.sum(
+                jnp.where(mine, exp_buf[which].astype(jnp.float32), 0.0), axis=-1, keepdims=True
+            )
+            power = jnp.broadcast_to(power, (n, hd))
+            scale_buf[which, 0] = jnp.exp2(-power)
+            scale_buf[which, 1] = jnp.exp2(power)
         for j in range(tokens // LANES):
-            piece = order_ref[:, j * LANES : (j + 1) * LANES]
+            piece = order_buf[j * LANES : (j + 1) * LANES].reshape(1, LANES)
             pos_buf[j * LANES : (j + 1) * LANES, :] = jnp.transpose(
                 jnp.broadcast_to(piece, (LANES, LANES))
             )
@@ -157,14 +193,16 @@
             swapped = jnp.where(even, pltpu.roll(x, hd - 1, 1), pltpu.roll(x, 1, 1))
             return (x * cosine + swapped * sine).astype(jnp.bfloat16)
 
-        def rebuilt(fresh, base, exponent):
-            power = jnp.full((1, hd), exponent, jnp.int32).astype(jnp.float32)
-            coded = jnp.clip((fresh - base) * jnp.exp2(-power), -clip_bound, clip_bound)
+        def rebuilt(fresh, base, which, b):
+            down = scale_buf[which, 0, pl.ds(b, 1), :]
+            up = scale_buf[which, 1, pl.ds(b, 1), :]
+            coded = jnp.clip((fresh - base) * down, -clip_bound, clip_bound)
             coded = coded.astype(jnp.bfloat16).astype(jnp.float32)
-            return (base + coded * jnp.exp2(power)).astype(jnp.bfloat16)
+            return (base + coded * up).astype(jnp.bfloat16)
 
         @pl.loop(0, n)
-        def _(b):
+        def _(i):
+            b = (i + jnp.where(lower, 0, n // 2)) % n
             for c in range(cores):
                 block = b * cores + c
 
@@ -178,21 +216,24 @@
                 k_raw = recv_buf[block, 0].astype(jnp.float32)
                 v_raw = recv_buf[block, 1].astype(jnp.float32)
                 q_raw = recv_buf[block, 2].astype(jnp.float32)
-                q_buf[where, :] = normed_rotated(q_raw, qg_ref[...], cosine, sine)
-                fresh = normed_rotated(k_raw, kg_ref[...], cosine, sine).astype(jnp.float32)
+                q_buf[where, :] = normed_rotated(q_raw, gain_buf[0], cosine, sine)
+                fresh = normed_rotated(k_raw, gain_buf[1], cosine, sine).astype(jnp.float32)
                 key_buf[where, :] = rebuilt(
-                    fresh, slot_base[where, :hd], exp_ref[0, my_head, b]
+                    fresh, slot_base[where, :hd], 0, b
                 )
                 val_buf[where, :] = rebuilt(
-                    v_raw, slot_base[where, hd:], exp_ref[1, my_head, b]
+                    v_raw, slot_base[where, hd:], 1, b
                 )
 
         tile = 2 * patch_rows
         per_tile = tile // rows
         score_scale = hd ** (-0.5)
 
-        @pl.loop(0, tokens // tile)
-        def _(t):
+        tiles = tokens // tile
+
+        @pl.loop(0, tiles)
+        def _(step):
+            t = jnp.where(lower, tiles - 1 - step, step)
             where = pl.ds(pl.multiple_of(t * tile, 16), tile)
             scores = lax.dot_general(
                 q_buf[where, :], key_buf[...], (((1,), (1,)), ((), ())),
@@ -244,14 +285,17 @@
     cores = lax.axis_size("head")
     blocks = n * cores
     tokens = blocks * rows
-    vmem = pl.BlockSpec(memory_space=pltpu.VMEM)
     return pl.pallas_call(
         functools.partial(kernel, (n, cores, heads // cores, rows)),
         out_shape=jax.ShapeDtypeStruct(q_raw.shape, jnp.bfloat16),
-        in_specs=[vmem] * 5
-        + [pl.BlockSpec(memory_space=pltpu.SMEM), vmem, pl.BlockSpec(memory_space=pl.ANY)],
-        out_specs=vmem,
+        in_specs=[pl.BlockSpec(memory_space=pltpu.HBM)] * 8,
+        out_specs=pl.BlockSpec(memory_space=pltpu.VMEM),
         scratch_shapes=[
+            pltpu.VMEM((3, rows, heads * hd), jnp.bfloat16),
+            pltpu.VMEM((2, 1, hd), jnp.float32),
+            pltpu.VMEM((2, n, heads), jnp.int32),
+            pltpu.VMEM((tokens,), jnp.int32),
+            pltpu.VMEM((2, 2, n, hd), jnp.float32),
             pltpu.VMEM((heads, 3, rows, hd), jnp.bfloat16),
             pltpu.VMEM((blocks, 3, rows, hd), jnp.bfloat16),
             pltpu.VMEM((tokens, 2 * hd), jnp.bfloat16),
@@ -264,6 +308,8 @@
             pltpu.VMEM((tokens, hd), jnp.bfloat16),
             pltpu.VMEM((blocks, rows, hd), jnp.bfloat16),
             pltpu.VMEM((heads, rows, hd), jnp.bfloat16),
+            pltpu.SemaphoreType.DMA((3,)),
+            pltpu.SemaphoreType.DMA((4,)),
             pltpu.SemaphoreType.DMA((2,)),
             pltpu.SemaphoreType.DMA((heads,)),
             pltpu.SemaphoreType.DMA((blocks,)),
@@ -271,11 +317,11 @@
             pltpu.SemaphoreType.DMA((heads,)),
         ],
         compiler_params=pltpu.CompilerParams(
-            collective_id=0, has_side_effects=True, vmem_limit_bytes=40 * 2**20
+            collective_id=0, has_side_effects=True, vmem_limit_bytes=64 * 2**20 - 2**17
         ),
     )(
-        q_raw, k_raw, v_raw, q_gain.reshape(1, hd), k_gain.reshape(1, hd), exponents,
-        order.reshape(1, tokens), base_kv,
+        q_raw, k_raw, v_raw, q_gain.reshape(1, hd), k_gain.reshape(1, hd),
+        exponents.transpose(0, 2, 1), order, base_kv,
     )
 
 

time: 33.7 us -> 28.4 us (0.84)
  local copies, waits for them, and re-layouts: 7.84 us -> 1.58 us
  Pallas kernels: 25.3 us -> 26.6 us
    unnamed x14 -> x1, local copies, waits for them, and re-layouts: 7.15 us -> 1.58 us
    pallas_call x1, Pallas kernels: 25.3 us -> 26.6 us  [per_device(): pl.pallas_call(functools.partial(kernel, (n, cores, heads // cores, rows)...]
    reshape x1 -> x0, local copies, waits for them, and re-layouts: 0.69 us -> none  [per_device(): order.reshape(1, tokens)]
where the time goes in v2:
time: 28.4 us; the launch traced here: 28.2 us
  Pallas kernels  26.6 us (94%)
  local copies, waits for them, and re-layouts  1.58 us (6%)
    pallas_call x1, Pallas kernels, per_device(): pl.pallas_call(functools.partial(kernel, (n, cores, heads // cores, rows)...  26.6 us
    unnamed x1, local copies, waits for them, and re-layouts  1.58 us

profile of v2, /device:TPU:0, one launch (start us, length us, event | category | flops | bytes accessed | tf_op | source)
XLA Modules:
  0.0 28.2 jit_solution(4558621734243035094)
XLA Ops:
  0.0 26.6 %shard_map.82 = bf16[48,1536]{1,0:T(8,128)(2,1)} custom-call(bf16[48,1536]{1,0:T(8,128)(2,1)} %q_ref.1, bf16[48,1536]{1,0:T(8,128)(2,1)} %k_ref.1, bf16[48,1536]{1,0:T(8,128)(2,1)} %v_ref.1, f32[1,128]{1,0:T(1,128)} %bitcast.4, f32[1,128]{1,0:T(1,128)} %bitcast.5, s32[2,8,12]{2,1,0:T(8,128)} %bitcast.3, s32[768]{0:T(1024)} %order_ref.1, ...), custom_call_target="tpu_custom_call" | custom-call | tf_op jit(solution)/shard_map/pallas_call | solution.py:288
  26.6 1.6 %copy.10 = bf16[48,1536]{1,0:T(8,128)(2,1)} copy(bf16[48,1536]{1,0:T(8,128)(2,1)} %shard_map.82) | data formatting | bytes 294912

commit v3 on v2

--- a/solution.py
+++ b/solution.py
@@ -18,7 +18,7 @@
 def kernel(
     sizes, q_ref, k_ref, v_ref, qg_ref, kg_ref, exp_ref, order_ref, base_ref, out_ref,
     raw_buf, gain_buf, exp_buf, order_buf, scale_buf, send_buf, recv_buf, base_buf, pos_buf, slot_base, cos_buf, sin_buf,
-    q_buf, key_buf, val_buf, o_send, o_recv,
+    key_buf, val_buf, o_send, o_recv,
     in_sem, small_sem, base_sem, send_sem, recv_sem, osend_sem, orecv_sem,
 ):
     n, cores, local_heads, rows = sizes
@@ -41,12 +41,13 @@
     def head_device(head):
         return {"patch": first_worker + head % local_heads, "head": head // local_heads}
 
-    def in_copy(head, block):
+    def in_copy(part, head, block):
+        which = pl.ds(0, 2) if part == 0 else pl.ds(2, 1)
         return pltpu.make_async_remote_copy(
-            src_ref=send_buf.at[head],
-            dst_ref=recv_buf.at[block],
-            send_sem=send_sem.at[head],
-            recv_sem=recv_sem.at[block],
+            src_ref=send_buf.at[head, which],
+            dst_ref=recv_buf.at[block, which],
+            send_sem=send_sem.at[part, head],
+            recv_sem=recv_sem.at[part, block],
             device_id=head_device(head),
             device_id_type=pl.DeviceIdType.MESH,
         )
@@ -119,18 +120,19 @@
 
     lower = patch < n // 2
     half_heads = local_heads // 2
-    for step in range(local_heads):
-        if local_heads % 2 == 0:
-            across = (step < half_heads) == lower
-            target = (patch + step) % half_heads + jnp.where(across, half_heads, 0)
-        else:
-            target = (patch + step) % local_heads
-        for c in range(cores):
-            head = ((core + c) % cores) * local_heads + target
-
-            @pl.when(jnp.logical_not(is_mine(head)))
-            def _():
-                in_copy(head, me).start()
+    for part in range(2):
+        for step in range(local_heads):
+            if local_heads % 2 == 0:
+                far = (step < half_heads) == (part == 0)
+                target = (patch + step) % half_heads + jnp.where(lower == far, half_heads, 0)
+            else:
+                target = (patch + step) % local_heads
+            for c in range(cores):
+                head = ((core + c) % cores) * local_heads + target
+
+                @pl.when(jnp.logical_not(is_mine(head)))
+                def _():
+                    in_copy(part, head, me).start()
 
     @pl.when(is_worker)
     def _():
@@ -208,15 +210,13 @@
 
                 @pl.when(block != me)
                 def _():
-                    in_copy(my_head, block).wait_recv()
+                    in_copy(0, my_head, block).wait_recv()
 
                 where = pl.ds(pl.multiple_of(block * rows, 16), rows)
                 cosine = cos_buf[where, :]
                 sine = sin_buf[where, :]
                 k_raw = recv_buf[block, 0].astype(jnp.float32)
                 v_raw = recv_buf[block, 1].astype(jnp.float32)
-                q_raw = recv_buf[block, 2].astype(jnp.float32)
-                q_buf[where, :] = normed_rotated(q_raw, gain_buf[0], cosine, sine)
                 fresh = normed_rotated(k_raw, gain_buf[1], cosine, sine).astype(jnp.float32)
                 key_buf[where, :] = rebuilt(
                     fresh, slot_base[where, :hd], 0, b
@@ -233,10 +233,21 @@
 
         @pl.loop(0, tiles)
         def _(step):
-            t = jnp.where(lower, tiles - 1 - step, step)
+            t = (step + jnp.where(lower, 0, tiles // 2)) % tiles
             where = pl.ds(pl.multiple_of(t * tile, 16), tile)
+            for i in range(per_tile):
+                block = t * per_tile + i
+
+                @pl.when(block != me)
+                def _():
+                    in_copy(1, my_head, block).wait_recv()
+
+            q_raw = jnp.concatenate(
+                [recv_buf[t * per_tile + i, 2] for i in range(per_tile)], axis=0
+            ).astype(jnp.float32)
+            queries = normed_rotated(q_raw, gain_buf[0], cos_buf[where, :], sin_buf[where, :])
             scores = lax.dot_general(
-                q_buf[where, :], key_buf[...], (((1,), (1,)), ((), ())),
+                queries, key_buf[...], (((1,), (1,)), ((), ())),
                 preferred_element_type=jnp.float32,
             ) * score_scale
             weights = jnp.exp(scores - jnp.max(scores, axis=-1, keepdims=True))
@@ -266,7 +277,8 @@
     def _(head):
         @pl.when(jnp.logical_not(is_mine(head)))
         def _():
-            in_copy(head, me).wait_send()
+            in_copy(0, head, me).wait_send()
+            in_copy(1, head, me).wait_send()
 
     @pl.when(is_worker)
     def _():
@@ -305,14 +317,13 @@
             pltpu.VMEM((tokens, hd), jnp.float32),
             pltpu.VMEM((tokens, hd), jnp.bfloat16),
             pltpu.VMEM((tokens, hd), jnp.bfloat16),
-            pltpu.VMEM((tokens, hd), jnp.bfloat16),
             pltpu.VMEM((blocks, rows, hd), jnp.bfloat16),
             pltpu.VMEM((heads, rows, hd), jnp.bfloat16),
             pltpu.SemaphoreType.DMA((3,)),
             pltpu.SemaphoreType.DMA((4,)),
             pltpu.SemaphoreType.DMA((2,)),
-            pltpu.SemaphoreType.DMA((heads,)),
-            pltpu.SemaphoreType.DMA((blocks,)),
+            pltpu.SemaphoreType.DMA((2, heads)),
+            pltpu.SemaphoreType.DMA((2, blocks)),
             pltpu.SemaphoreType.DMA((blocks,)),
             pltpu.SemaphoreType.DMA((heads,)),
         ],

time: 28.4 us -> 26.1 us (0.919)
  the two profiles are of different devices: /device:TPU:0 before, /device:TPU:27 now
where the time goes in v3:
time: 26.1 us; the launch traced here: 26 us
  Pallas kernels  24.4 us (93%)
  local copies, waits for them, and re-layouts  1.58 us (6%)
    pallas_call x1, Pallas kernels, per_device(): pl.pallas_call(functools.partial(kernel, (n, cores, heads // cores, rows)...  24.4 us
    unnamed x1, local copies, waits for them, and re-layouts  1.58 us

profile of v3, /device:TPU:27, one launch (start us, length us, event | category | flops | bytes accessed | tf_op | source)
XLA Modules:
  0.0 26.0 jit_solution(16154372743590838926)
XLA Ops:
  0.0 24.4 %shard_map.82 = bf16[48,1536]{1,0:T(8,128)(2,1)} custom-call(bf16[48,1536]{1,0:T(8,128)(2,1)} %q_ref.1, bf16[48,1536]{1,0:T(8,128)(2,1)} %k_ref.1, bf16[48,1536]{1,0:T(8,128)(2,1)} %v_ref.1, f32[1,128]{1,0:T(1,128)} %bitcast.4, f32[1,128]{1,0:T(1,128)} %bitcast.5, s32[2,8,12]{2,1,0:T(8,128)} %bitcast.3, s32[768]{0:T(1024)} %order_ref.1, ...), custom_call_target="tpu_custom_call" | custom-call | tf_op jit(solution)/shard_map/pallas_call | solution.py:300
  24.4 1.6 %copy.10 = bf16[48,1536]{1,0:T(8,128)(2,1)} copy(bf16[48,1536]{1,0:T(8,128)(2,1)} %shard_map.82) | data formatting | bytes 294912

commit v4 on v3

--- a/solution.py
+++ b/solution.py
@@ -123,7 +123,7 @@
     for part in range(2):
         for step in range(local_heads):
             if local_heads % 2 == 0:
-                far = (step < half_heads) == (part == 0)
+                far = step < half_heads
                 target = (patch + step) % half_heads + jnp.where(lower == far, half_heads, 0)
             else:
                 target = (patch + step) % local_heads
@@ -233,7 +233,7 @@
 
         @pl.loop(0, tiles)
         def _(step):
-            t = (step + jnp.where(lower, 0, tiles // 2)) % tiles
+            t = (step + jnp.where(lower, tiles // 2, 0)) % tiles
             where = pl.ds(pl.multiple_of(t * tile, 16), tile)
             for i in range(per_tile):
                 block = t * per_tile + i

time: 26.1 us -> 25.9 us (level)
  the two profiles are of different devices: /device:TPU:27 before, /device:TPU:0 now
where the time goes in v4:
time: 25.9 us; the launch traced here: 25.7 us
  Pallas kernels  24.2 us (93%)
  local copies, waits for them, and re-layouts  1.58 us (6%)
    pallas_call x1, Pallas kernels, per_device(): pl.pallas_call(functools.partial(kernel, (n, cores, heads // cores, rows)...  24.2 us
    unnamed x1, local copies, waits for them, and re-layouts  1.58 us

profile of v4, /device:TPU:0, one launch (start us, length us, event | category | flops | bytes accessed | tf_op | source)
XLA Modules:
  0.0 25.7 jit_solution(11738504560233052295)
XLA Ops:
  0.0 24.2 %shard_map.82 = bf16[48,1536]{1,0:T(8,128)(2,1)} custom-call(bf16[48,1536]{1,0:T(8,128)(2,1)} %q_ref.1, bf16[48,1536]{1,0:T(8,128)(2,1)} %k_ref.1, bf16[48,1536]{1,0:T(8,128)(2,1)} %v_ref.1, f32[1,128]{1,0:T(1,128)} %bitcast.4, f32[1,128]{1,0:T(1,128)} %bitcast.5, s32[2,8,12]{2,1,0:T(8,128)} %bitcast.3, s32[768]{0:T(1024)} %order_ref.1, ...), custom_call_target="tpu_custom_call" | custom-call | tf_op jit(solution)/shard_map/pallas_call | solution.py:300
  24.2 1.6 %copy.10 = bf16[48,1536]{1,0:T(8,128)(2,1)} copy(bf16[48,1536]{1,0:T(8,128)(2,1)} %shard_map.82) | data formatting | bytes 294912
